TPU v7x, 512 devices: a whole 4x8x8 slice. The times are simulated.
512 devices in a mesh: shard: 128 (over y, z, core), grp: 4 (over x).
Axes of the slice: x: 4, y: 8, z: 8, core: 2. Of those that a mesh axis runs over, the one named last changes fastest.
Arguments:
- embeddings: bfloat16 [262144, 768], P(('shard', 'grp')), may hold values from -18 to 18
- cluster_id: int32 [262144], P(('shard', 'grp')), may hold values from 0 to 1001
- row_targets: int32 [262144, 3], P(('shard', 'grp')), may hold values from -1 to 511, as said below
Outputs:
- nearest_similarity: float32 [262144], P(('shard', 'grp'))
Inputs may be any that keep to these rules, and one draw needn't show every extreme that they name: `row_targets`: each row names 1 to 3 distinct devices and -1 in its other entries. Among the rows of one device at most 2 entries name one device, and some device is named by exactly 2 entries of every device's rows.
All inputs are finite; a program needn't handle non-finite values.
Results may differ from a plain program's by a relative error of at most 0.00069.
Values may be sent and summed in bfloat16 or wider, within the bound.
A program may use at most 64 MiB of HBM per device.

v0:
```python
import jax
import jax.numpy as jnp
from jax import lax
from jax.sharding import PartitionSpec as P


def slot_places(targets, devices, capacity):
    count = targets.shape[0]
    keyed = jnp.where(targets >= 0, targets, devices)
    order = jnp.argsort(keyed, stable=True)
    ordered = keyed[order]
    positions = jnp.arange(count, dtype=jnp.int32)
    fresh = jnp.concatenate([jnp.ones((1,), jnp.bool_), ordered[1:] != ordered[:-1]])
    first = lax.cummax(jnp.where(fresh, positions, 0), axis=0)
    ranks = jnp.zeros((count,), jnp.int32).at[order].set(positions - first)
    return jnp.where(targets >= 0, targets * capacity + ranks, -1)


def square_maxima(members, member_tags):
    total = members.shape[0]
    features = members.shape[1]
    blocks_count = total // 512
    positions = jnp.arange(total, dtype=jnp.int32)
    stacked = (
        members.reshape(blocks_count, 512, features),
        member_tags.reshape(blocks_count, 512),
        positions.reshape(blocks_count, 512),
    )

    def advance(highest, portion):
        block_rows, block_tags, block_positions = portion
        scores = lax.dot_general(
            members, block_rows, (((1,), (1,)), ((), ())), preferred_element_type=jnp.float32
        )
        allowed = (member_tags[:, None] == block_tags[None, :]) & (
            positions[:, None] != block_positions[None, :]
        )
        return (
            jnp.maximum(highest, jnp.max(jnp.where(allowed, scores, jnp.float32(-1.0)), axis=1)),
            None,
        )

    highest, unused = lax.scan(advance, jnp.full((total,), -1.0, jnp.float32), stacked)
    return highest


def body(embeddings, cluster_id, row_targets):
    local_rows = embeddings.shape[0]
    features = embeddings.shape[1]
    copies = row_targets.shape[1]
    shards = lax.axis_size("shard")
    groups = lax.axis_size("grp")
    devices = shards * groups
    bucket = 2 * local_rows
    capacity = bucket // devices
    values = embeddings.astype(jnp.float32)
    squares = jnp.sum(values * values, axis=1, keepdims=True)
    normed = (values * lax.rsqrt(squares + 1e-06)).astype(jnp.bfloat16)
    places = slot_places(row_targets.reshape(-1), devices, capacity).reshape(local_rows, copies)
    shard_rows, shard_places, shard_tags = (
        lax.all_gather(normed, "grp", axis=0, tiled=True),
        lax.all_gather(places, "grp", axis=0, tiled=True),
        lax.all_gather(cluster_id, "grp", axis=0, tiled=True),
    )
    total_rows = groups * local_rows
    source_group = (jnp.arange(total_rows, dtype=jnp.int32) // local_rows)[:, None]
    target_device = jnp.where(shard_places >= 0, shard_places // capacity, 0)
    wanted = (shard_places >= 0) & (target_device % groups == lax.axis_index("grp"))
    buffer_slot = (
        target_device // groups * (groups * capacity)
        + source_group * capacity
        + shard_places % capacity
    )
    buffer_slot = jnp.where(wanted, buffer_slot, bucket).astype(jnp.int32)
    row_number = jnp.broadcast_to(
        jnp.arange(total_rows, dtype=jnp.int32)[:, None], buffer_slot.shape
    )
    source_row = (
        jnp.full((bucket,), -1, jnp.int32)
        .at[buffer_slot.reshape(-1)]
        .set(row_number.reshape(-1), mode="drop")
    )
    filled = source_row >= 0
    picked = jnp.maximum(source_row, 0)
    sent_rows = jnp.where(filled[:, None], shard_rows[picked], jnp.zeros((), jnp.bfloat16))
    sent_tags = jnp.where(filled, shard_tags[picked], -1).astype(jnp.int32)
    got_rows, got_tags = (
        lax.all_to_all(
            sent_rows.reshape(shards, groups * capacity, features),
            "shard",
            split_axis=0,
            concat_axis=0,
            tiled=True,
        ),
        lax.all_to_all(
            sent_tags.reshape(shards, groups * capacity),
            "shard",
            split_axis=0,
            concat_axis=0,
            tiled=True,
        ),
    )
    members = got_rows.reshape(bucket, features)
    raw_tags = got_tags.reshape(bucket)
    lone_tags = -2 - jnp.arange(bucket, dtype=jnp.int32)
    member_tags = jnp.where(raw_tags >= 0, raw_tags, lone_tags).astype(jnp.int32)
    highest = square_maxima(members, member_tags)
    returned = lax.all_to_all(
        lax.all_to_all(
            highest.reshape(shards, groups, capacity),
            "shard",
            split_axis=0,
            concat_axis=0,
            tiled=True,
        ),
        "grp",
        split_axis=1,
        concat_axis=1,
        tiled=True,
    )
    flat_maxima = returned.reshape(-1)
    found = jnp.where(places >= 0, flat_maxima[jnp.maximum(places, 0)], jnp.float32(-1.0))
    return jnp.max(found, axis=1)


def solution(mesh):
    placed = (P(("shard", "grp"), None), P(("shard", "grp")), P(("shard", "grp"), None))
    return jax.shard_map(
        body, mesh=mesh, in_specs=placed, out_specs=P(("shard", "grp")), check_vma=False
    )
```

profile of v0, /device:TPU:1, one launch (start us, length us, event | category | flops | bytes accessed | tf_op | source)
XLA Modules:
  0.0 224.5 jit_solution(17040334699551554809)
XLA Ops:
  6.5 1.4 fusion.7
  7.9 2.2 fusion.8
  10.6 5.0 %sort.17 = (s32[1536]{0:T(1024)}, s32[1536]{0:T(1024)S(1)}) sort(s32[1536]{0:T(1024)S(1)} %compare_select_fusion.5, s32[1536]{0:T(1024)S(1)} %iota.58), dimensions={0}, to_apply=%region_0.0 | sort | flops 16896 | bytes 24576 | tf_op jit(solution)/shard_map/jit(argsort)/sort | solution.py:10
  15.6 8.4 %gather_fusion = s32[1536]{0:T(1024)S(1)} fusion(s32[1536]{0:T(1024)S(1)} %compare_select_fusion.5, s32[2048]{0:T(1024)S(1)} %pad_clamp_fusion.1), kind=kCustom, calls=%fused_computation | custom fusion | bytes 18432 | tf_op jit(solution)/shard_map/gather | solution.py:11
  24.7 6.2 %scatter_custom_fusion = s32[1536]{0:T(1024)S(1)} fusion(s32[1536]{0:T(1024)S(1)} %compare_select_fusion.1, s32[1536]{0:T(1024)S(1)} %bitcast_subtract_fusion, s32[]{:T(128)} %constant.100.clone.1), kind=kCustom, calls=%fused_computation.69 | custom fusion | bytes 6148 | tf_op jit(solution)/shard_map/scatter | solution.py:15
  31.2 21.0 %all_gather.9 = s32[2048,3]{1,0:T(8,128)S(1)} all-gather(s32[512,3]{1,0:T(8,128)S(1)} %reshape.124), channel_id=1, replica_groups=mesh['shard'=128,'grp'=4] {'grp'}, dimensions={0}, use_global_device_ids=true | all-gather | bytes 30720 | tf_op jit(solution)/shard_map/all_gather | solution.py:62
  52.2 2.1 fusion.14
  54.2 0.7 reshape.125
  55.1 0.7 reshape.176
  55.8 23.0 %scatter_custom_fusion.1 = s32[1024]{0:T(1024)S(1)} fusion(s32[6144]{0:T(1024)S(1)} %bitcast.45, s32[6144]{0:T(1024)S(1)} %reshape.176, s32[]{:T(128)} %constant.107.clone.1), kind=kCustom, calls=%fused_computation.74 | custom fusion | bytes 4100 | tf_op jit(solution)/shard_map/scatter | solution.py:81
  78.7 8.1 %all-gather = s32[4,1,512]{2,1,0:T(1,128)S(1)} all-gather(s32[1,1,512]{2,1,0:T(1,128)S(1)} %bitcast.46), channel_id=1, replica_groups=mesh['shard'=128,'grp'=4] {'grp'}, dimensions={0}, use_global_device_ids=true | all-gather | bytes 10240 | tf_op jit(solution)/shard_map/all_gather | solution.py:63
  86.8 6.2 %gather_fusion.1 = s32[1024]{0:T(1024)S(1)} fusion(s32[2048]{0:T(1024)S(1)} %bitcast.37, s32[1024]{0:T(1024)S(1)} %maximum_clamp_fusion), kind=kCustom, calls=%fused_computation.1 | custom fusion | bytes 12288 | tf_op jit(solution)/shard_map/gather | solution.py:86
  93.0 0.7 all_to_all.15
  93.7 21.9 %all-to-all-start = ((s32[128,1,8]{2,1,0:T(1,128)}), s32[128,1,8]{2,1,0:T(1,128)S(1)}, u32[]{:S(2)}, u32[]{:S(2)}) async-start(s32[128,1,8]{2,1,0:T(1,128)} %bitcast.5), calls=%async_computation | async-start | bytes 131072 | tf_op jit(solution)/shard_map/all_to_all | solution.py:95
  115.8 6.8 %gather_fusion.2 = bf16[1024,768]{1,0:T(8,128)(2,1)S(1)} fusion(bf16[2048,768]{1,0:T(8,128)(2,1)} %all-gather.3.cloned.1.call-done, s32[1024]{0:T(1024)S(1)} %maximum_clamp_fusion), kind=kCustom, calls=%fused_computation.2 | custom fusion | bytes 3149824 | tf_op jit(solution)/shard_map/gather | solution.py:85
  122.5 1.4 bitcast_select_fusion.1
  123.9 3.2 %all-to-all-done = s32[128,1,8]{2,1,0:T(1,128)S(1)} async-done(((s32[128,1,8]{2,1,0:T(1,128)}), s32[128,1,8]{2,1,0:T(1,128)S(1)}, u32[]{:S(2)}, u32[]{:S(2)}) %all-to-all-start) | async-done | bytes 4128 | tf_op jit(solution)/shard_map/all_to_all | solution.py:95
  127.1 10.5 %all-to-all-start.1 = ((bf16[128,8,768]{2,1,0:T(8,128)(2,1)}), bf16[128,8,768]{2,1,0:T(8,128)(2,1)S(1)}, u32[]{:S(2)}, u32[]{:S(2)}) async-start(bf16[128,8,768]{2,1,0:T(8,128)(2,1)} %bitcast_select_fusion.1), calls=%async_computation.1 | async-start | bytes 3145728 | tf_op jit(solution)/shard_map/all_to_all | solution.py:88
  137.8 0.5 broadcast.167
  138.3 0.8 reduce.7
  139.2 39.6 %all-to-all-done.1 = bf16[128,8,768]{2,1,0:T(8,128)(2,1)S(1)} async-done(((bf16[128,8,768]{2,1,0:T(8,128)(2,1)}), bf16[128,8,768]{2,1,0:T(8,128)(2,1)S(1)}, u32[]{:S(2)}, u32[]{:S(2)}) %all-to-all-start.1) | async-done | bytes 1572896 | tf_op jit(solution)/shard_map/all_to_all | solution.py:88
  178.7 2.4 %while.11 = (s32[]{:T(128)}, f32[1024]{0:T(1024)S(1)}, s32[1024]{0:T(1024)S(1)}, s32[2,512]{1,0:T(2,128)S(1)}, s32[2,512]{1,0:T(2,128)S(1)}, /*index=5*/bf16[2,5...) while((s32[]{:T(128)}, f32[1024]{0:T(1024)S(1)}, ...), condition=%wide.region_8.9_spmd.clone, body=%wide.region_6.8_spmd.clone.sunk | while | flops 807928832 | bytes 2392183 | solution.py:43
  178.8 1.1 fusion.33
  179.9 1.1 fusion.33
  181.1 0.3 reshape.130
  181.4 0.9 copy.7
  182.3 19.9 %all_to_all.24 = f32[128,4,2]{1,2,0:T(2,128)S(1)} all-to-all(f32[128,4,2]{1,2,0:T(2,128)S(1)} %copy.7), channel_id=1, replica_groups=mesh['shard'=128,'grp'=4] {'shard'}, dimensions={0} | all-to-all | bytes 8192 | tf_op jit(solution)/shard_map/all_to_all | solution.py:109
  202.2 0.7 copy.8
  202.9 3.4 %all-to-all-start.3 = ((f32[128,4,2]{0,2,1:T(2,128)}), f32[128,4,2]{0,2,1:T(2,128)S(1)}, u32[]{:S(2)}, u32[]{:S(2)}) async-start(f32[128,4,2]{0,2,1:T(2,128)} %copy.8), calls=%async_computation.3 | async-start | bytes 8192 | tf_op jit(solution)/shard_map/all_to_all | solution.py:108
  206.3 4.1 %all-to-all-done.3 = f32[128,4,2]{0,2,1:T(2,128)S(1)} async-done(((f32[128,4,2]{0,2,1:T(2,128)}), f32[128,4,2]{0,2,1:T(2,128)S(1)}, u32[]{:S(2)}, u32[]{:S(2)}) %all-to-all-start.3) | async-done | bytes 4128 | tf_op jit(solution)/shard_map/all_to_all | solution.py:108
  210.9 5.8 %gather_fusion.3 = f32[1536]{0:T(1024)S(1)} fusion(f32[1024]{0:T(1024)S(1)} %reshape.131, s32[2048]{0:T(1024)S(1)} %pad_clamp_fusion), kind=kCustom, calls=%fused_computation.3 | custom fusion | bytes 18432 | tf_op jit(solution)/shard_map/gather | solution.py:122
  216.9 0.7 select_reduce_fusion
  (42 shorter events, 2.4 us)
Async XLA Ops:
  6.5 3.6 %copy-start = (s32[512,3]{0,1:T(4,128)S(1)}, s32[512,3]{0,1:T(4,128)}, u32[]{:S(2)}) copy-start(s32[512,3]{0,1:T(4,128)} %param.7) | copy-start | bytes 18436
  6.5 109.2 %all-gather.3.cloned.1.call-start = ((), (), s32[]{:S(2)}) async-start(), calls=%async_computation.4 | async-start | bytes 3932160 | tf_op jit(solution)/shard_map/all_gather | solution.py:61
  54.2 24.5 %copy-start.1 = (s32[512]{0:T(512)S(1)}, s32[512]{0:T(512)}, u32[]{:S(2)}) copy-start(s32[512]{0:T(512)} %param.6) | copy-start | bytes 6148
  93.7 33.4 %all-to-all-start = ((s32[128,1,8]{2,1,0:T(1,128)}), s32[128,1,8]{2,1,0:T(1,128)S(1)}, u32[]{:S(2)}, u32[]{:S(2)}) async-start(s32[128,1,8]{2,1,0:T(1,128)} %bitcast.5), calls=%async_computation | async-start | bytes 131072 | tf_op jit(solution)/shard_map/all_to_all | solution.py:95
  127.1 51.6 %all-to-all-start.1 = ((bf16[128,8,768]{2,1,0:T(8,128)(2,1)}), bf16[128,8,768]{2,1,0:T(8,128)(2,1)S(1)}, u32[]{:S(2)}, u32[]{:S(2)}) async-start(bf16[128,8,768]{2,1,0:T(8,128)(2,1)} %bitcast_select_fusion.1), calls=%async_computation.1 | async-start | bytes 3145728 | tf_op jit(solution)/shard_map/all_to_all | solution.py:88
  202.9 7.5 %all-to-all-start.3 = ((f32[128,4,2]{0,2,1:T(2,128)}), f32[128,4,2]{0,2,1:T(2,128)S(1)}, u32[]{:S(2)}, u32[]{:S(2)}) async-start(f32[128,4,2]{0,2,1:T(2,128)} %copy.8), calls=%async_computation.3 | async-start | bytes 8192 | tf_op jit(solution)/shard_map/all_to_all | solution.py:108
Sparse Core Ops, SparseCore 0:
  10.3 58.7 all-gather.2
where the time goes:
time: 225 us
  local copies, waits for them, and re-layouts  62.6 us (28%)
  blocking collectives  49 us (22%)
  waiting for transfers between devices  46.9 us (21%)
  starting transfers between devices  35.9 us (16%)
  other arithmetic  14.2 us (6%)
  between operations  13.7 us (6%)
  matrix products  2.27 us (1%)
    all_to_all x1, waiting for transfers between devices, body(): lax.all_to_all(sent_rows.reshape(shards, groups * capacity, features), 's...  39.6 us
    scatter x1, local copies, waits for them, and re-layouts, body(): source_row = jnp.full((bucket,), -1, jnp.int32).at[buffer_slot.reshape(-1...  23 us
    all_to_all x1, starting transfers between devices, body(): lax.all_to_all(sent_tags.reshape(shards, groups * capacity), 'shard', spl...  21.9 us
    all_gather x1, blocking collectives, body(): lax.all_gather(places, 'grp', axis=0, tiled=True)  21 us
    all_to_all x1, blocking collectives, body(): lax.all_to_all(highest.reshape(shards, groups, capacity), 'shard', split_...  19.9 us
    all_to_all x1, starting transfers between devices, body(): lax.all_to_all(sent_rows.reshape(shards, groups * capacity, features), 's...  10.5 us
    gather x1, local copies, waits for them, and re-layouts, slot_places(): ordered = keyed[order]  8.39 us
    all_gather x1, blocking collectives, body(): lax.all_gather(cluster_id, 'grp', axis=0, tiled=True)  8.08 us
  transfers between devices with their start and end apart: 4, of which 3 were waited for; matrix products, arithmetic and copies ran while one was open for 28% of the time, Pallas kernels for 0%

commit v1 on v0

v1 whole, which is shorter than its diff:
```python
import jax
import jax.numpy as jnp
from jax import lax
from jax.experimental import pallas as pl
from jax.experimental.pallas import tpu as pltpu
from jax.sharding import PartitionSpec as P

MESH = pl.DeviceIdType.MESH
SIDE = 8
CORES = 2
SHARDS = SIDE * SIDE * CORES
GROUPS = 4
CAP = 2
PAIR = GROUPS * CAP
LANES = 128
CHUNK = 16
CHUNKS = SHARDS // CHUNK
ORDER = (4, 5, 0, 1, 2, 3, 6, 7)
EARLY = 2
TAGS_AFTER = 3
TURNS_AFTER = (4, 5)
SCORES_AFTER = (6, 7)
SCORED = (0, 32, 64, 96, 112, 128)


def sway(n):
    return (n + 1) // 2 * (n % 2 * 2 - 1) % SIDE


def steps(place):
    half = SIDE // 2
    chunk, pair, odd = place // CHUNK, place % CHUNK // 2, place % 2
    first = (chunk // CORES == 0) * 1
    sign = 1 - 2 * odd
    near, far = pair % half, pair // half
    dy = first * (sign * near + half * odd * ((near == 0) * 1)) + (1 - first) * sign * sway(pair)
    dz = dy + first * half * far + (1 - first) * sign * (chunk // CORES)
    return (dy + SIDE) % SIDE, (dz + 2 * SIDE) % SIDE, chunk % CORES


def shard_at(me, place, sign):
    dy, dz, dc = steps(place)
    y = (me // (SIDE * CORES) + sign * dy + SIDE) % SIDE
    z = ((me // CORES) % SIDE + sign * dz + SIDE) % SIDE
    c = (me + dc) % CORES
    return (y * SIDE + z) * CORES + c


def kernel(
    emb_hbm,
    cid_hbm,
    tgt_hbm,
    out_ref,
    emb_ref,
    cid_ref,
    tgt_ref,
    unit,
    hot,
    xsend,
    stage,
    ysend,
    recv,
    mid,
    tiles,
    tag_xs,
    ret_xs,
    tag_send,
    tag_recv,
    ret_send,
    ret_recv,
    peak,
    in_sem,
    xs_sem,
    xr_sem,
    ys_sem,
    yr_sem,
    tile_ss,
    tile_rs,
    row_ss,
    row_rs,
):
    rows, features = emb_ref.shape
    me = lax.axis_index("shard")
    grp = lax.axis_index("grp")
    f32 = jnp.float32
    bf16 = jnp.bfloat16

    incoming = [
        pltpu.make_async_copy(src, dst, in_sem.at[n])
        for n, (src, dst) in enumerate(
            [(tgt_hbm, tgt_ref), (cid_hbm, cid_ref), (emb_hbm, emb_ref)]
        )
    ]
    for copy in incoming:
        copy.start()

    ys = [(me // (SIDE * CORES) + d) % SIDE * (SIDE * CORES) for d in range(SIDE)]
    zs = [(me // CORES + d) % SIDE * CORES for d in range(SIDE)]
    cs = [(me + d) % CORES for d in range(CORES)]

    def at(dy, dz, dc):
        return {"shard": ys[dy % SIDE] + zs[dz % SIDE] + cs[dc]}

    def ahead(place):
        return at(*steps(place))

    def behind(place):
        dy, dz, dc = steps(place)
        return at(-dy, -dz, dc)

    def along(e):
        return {"grp": (grp + e + GROUPS) % GROUPS}

    barrier = pltpu.get_barrier_semaphore()
    for e in range(1, GROUPS):
        pl.semaphore_signal(
            barrier, inc=1, device_id=along(e), device_id_type=MESH
        )
    for place in range(1, SHARDS):
        pl.semaphore_signal(barrier, inc=1, device_id=ahead(place), device_id_type=MESH)

    place = lax.broadcasted_iota(jnp.int32, (SHARDS, 1), 0)
    peers = shard_at(me, place, 1) * GROUPS
    before = lax.broadcasted_iota(jnp.int32, (rows, rows), 0) < lax.broadcasted_iota(
        jnp.int32, (rows, rows), 1
    )
    before = jnp.where(before, 1.0, 0.0).astype(bf16)
    incoming[0].wait()
    named = []
    for e in range(GROUPS):
        target = peers + (grp + e) % GROUPS
        hit = tgt_ref[0:1, :] == target
        for c in range(1, tgt_ref.shape[0]):
            hit = hit | (tgt_ref[c : c + 1, :] == target)
        named.append(jnp.where(hit, 1.0, 0.0).astype(f32))
    named = jnp.concatenate(named, axis=0)
    rank = jnp.dot(named.astype(bf16), before, preferred_element_type=f32)
    for r in range(CAP):
        pick = jnp.where(rank == float(r), named, 0.0).astype(bf16)
        for e in range(GROUPS):
            hot[e * CAP + r] = pick[e * SHARDS : (e + 1) * SHARDS, :]

    incoming[2].wait()
    values = emb_ref[...].astype(f32)
    squares = jnp.sum(values * values, axis=1, keepdims=True)
    unit[...] = (values * lax.rsqrt(squares + 1e-06)).astype(bf16)

    size = PAIR * CHUNK
    order_out = lax.broadcasted_iota(jnp.int32, (size, size), 0)
    order_in = lax.broadcasted_iota(jnp.int32, (size, size), 1)
    turn = (order_in % CHUNK == order_out // PAIR) & (order_in // CHUNK == order_out % PAIR)
    turn = jnp.where(turn, 1.0, 0.0).astype(bf16)
    back = (order_out % CHUNK == order_in // PAIR) & (order_out // CHUNK == order_in % PAIR)
    back = jnp.where(back, 1.0, 0.0).astype(bf16)

    def by_place_first(block):
        block = jnp.dot(turn, block, preferred_element_type=f32).astype(bf16)
        return block.reshape(CHUNK, PAIR, features)

    def keep_for_x(k, j, block):
        e, r = j // CAP, j % CAP
        if e == 0:
            stage[k, 0, r * CHUNK : (r + 1) * CHUNK, :] = block
        else:
            xsend[k, e - 1, r * CHUNK : (r + 1) * CHUNK, :] = block

    def pack_rows(chunks):
        pick = [hot[j, k * CHUNK : (k + 1) * CHUNK, :] for k in chunks for j in range(PAIR)]
        packed = jnp.dot(
            jnp.concatenate(pick, axis=0), unit[...], preferred_element_type=f32
        ).astype(bf16)
        for n, k in enumerate(chunks):
            block = packed[n * size : (n + 1) * size, :]
            if k in ORDER[:EARLY]:
                ysend[k * CHUNK : (k + 1) * CHUNK] = by_place_first(block)
            else:
                for j in range(PAIR):
                    keep_for_x(k, j, block[j * CHUNK : (j + 1) * CHUNK, :])

    def x_copies(k):
        return [
            pltpu.make_async_remote_copy(
                src_ref=xsend.at[k, e - 1, pl.ds(r * CHUNK, CHUNK)],
                dst_ref=stage.at[k, e, pl.ds(r * CHUNK, CHUNK)],
                send_sem=xs_sem,
                recv_sem=xr_sem.at[k],
                device_id=along(e),
                device_id_type=MESH,
            )
            for r in range(CAP)
            for e in (1, 3, 2)
        ]

    def x_arrived(k):
        part = stage.at[k, pl.ds(1, GROUPS - 1)]
        pltpu.make_async_copy(part, part, xr_sem.at[k]).wait()
        return by_place_first(stage[k].reshape(size, features))

    def yz_arrived(k):
        first = max(1, k * CHUNK)
        part = pl.ds(first, (k + 1) * CHUNK - first)
        part = (mid if k in ORDER[:EARLY] else recv).at[part]
        pltpu.make_async_copy(part, part, yr_sem.at[k]).wait()

    def send_rows(n):
        k = ORDER[n]
        copies = [
            pltpu.make_async_remote_copy(
                src_ref=ysend.at[place],
                dst_ref=(mid if k in ORDER[:EARLY] else recv).at[place],
                send_sem=ys_sem,
                recv_sem=yr_sem.at[k],
                device_id=ahead(place),
                device_id_type=MESH,
            )
            for place in range(max(1, k * CHUNK), (k + 1) * CHUNK)
        ]
        if n + EARLY < CHUNKS:
            between = x_copies(ORDER[n + EARLY])
            for m, copy in enumerate(between):
                copies.insert(m + (m + 1) * CHUNK // (len(between) + 1), copy)
        for copy in copies:
            copy.start()

    def pass_rows(n):
        k = ORDER[n]
        ysend[k * CHUNK : (k + 1) * CHUNK] = x_arrived(k)
        if k == 0:
            recv[0] = ysend[0]
        send_rows(n)

    def turn_rows(k):
        yz_arrived(k)
        block = mid[k * CHUNK : (k + 1) * CHUNK].reshape(size, features)
        block = jnp.dot(back, block, preferred_element_type=f32).astype(bf16)
        for j in range(PAIR):
            keep_for_x(k, j, block[j * CHUNK : (j + 1) * CHUNK, :])
        for copy in x_copies(k):
            copy.start()

    pack_rows(ORDER[: 2 * EARLY])
    pl.semaphore_wait(barrier, SHARDS - 1 + GROUPS - 1)
    for n in range(EARLY):
        send_rows(n)
    pack_rows(ORDER[2 * EARLY :])

    row8 = lax.broadcasted_iota(jnp.int32, (PAIR, LANES), 0) // CAP

    def spread_tile(n, held, sign):
        for e in range(1, GROUPS):
            pltpu.make_async_remote_copy(
                src_ref=tiles.at[n],
                dst_ref=held.at[e - 1],
                send_sem=tile_ss.at[n],
                recv_sem=tile_rs.at[n],
                device_id=along(sign * e),
                device_id_type=MESH,
            ).start()

    def merge_tile(n, held):
        pltpu.make_async_copy(held, held, tile_rs.at[n]).wait()
        merged = tiles[n]
        for e in range(1, GROUPS):
            merged = jnp.where(row8 == e, held[e - 1], merged)
        return jnp.transpose(
            jnp.concatenate([merged, jnp.zeros((LANES - PAIR, LANES), f32)], axis=0)
        )

    others = pl.ds(1, SHARDS - 1)

    def spread_rows(n, sent, held, device):
        held[0] = sent[0]
        for place in range(1, SHARDS):
            pltpu.make_async_remote_copy(
                src_ref=sent.at[place],
                dst_ref=held.at[place],
                send_sem=row_ss.at[n],
                recv_sem=row_rs.at[n],
                device_id=device(place),
                device_id_type=MESH,
            ).start()

    def rows_arrived(n, held):
        pltpu.make_async_copy(held.at[others], held.at[others], row_rs.at[n]).wait()

    incoming[1].wait()
    cid = cid_ref[...].astype(f32) + 1.0
    lane = lax.broadcasted_iota(jnp.int32, (SHARDS, LANES), 1)
    tags = jnp.zeros((SHARDS, LANES), f32)
    for j in range(PAIR):
        tag = jnp.sum(hot[j].astype(f32) * cid, axis=1, keepdims=True)
        tags = jnp.where(lane == j, tag, tags)
    tiles[0] = jnp.transpose(tags)[0:PAIR, :] - 1.0
    spread_tile(0, tag_xs, 1)

    total = SHARDS * PAIR
    lanes = lax.broadcasted_iota(jnp.int32, (total, LANES), 1)
    member = lax.broadcasted_iota(jnp.int32, (total, LANES), 0)
    mine = lanes == member % PAIR
    number = lax.broadcasted_iota(jnp.int32, (total, 1), 0)
    column = lax.broadcasted_iota(jnp.int32, (1, total), 1)

    def member_tags():
        rows_arrived(0, tag_recv)
        spread = jnp.broadcast_to(tag_recv[...], (SHARDS, PAIR, LANES)).reshape(total, LANES)
        tag_col = jnp.sum(jnp.where(mine, spread, 0.0), axis=1, keepdims=True)
        tag_col = jnp.where(tag_col < 0.0, -2.0 - number.astype(f32), tag_col)
        return tag_col, jnp.transpose(jnp.broadcast_to(tag_col, (total, LANES)))[0:1, :]

    def fold(scores):
        best = scores[:, 0:LANES]
        for first in range(LANES, scores.shape[1], LANES):
            best = jnp.maximum(best, scores[:, first : first + LANES])
        return best

    def score(begin, end):
        for k in range(begin // CHUNK, end // CHUNK):
            if k in ORDER[:EARLY]:
                recv[k * CHUNK : (k + 1) * CHUNK] = x_arrived(k)
            else:
                yz_arrived(k)
        low, high = begin * PAIR, end * PAIR
        scores = lax.dot_general(
            recv[0:end].reshape(high, features),
            recv[begin:end].reshape(high - low, features),
            (((1,), (1,)), ((), ())),
            preferred_element_type=f32,
        )
        scores = jnp.where(tag_col[0:high, :] == tag_row[:, low:high], scores, -1.0)
        own = scores[low:high, :]
        own = fold(jnp.where(number[low:high, :] != column[:, low:high], own, -1.0))
        if low:
            past = scores[0:low, :]
            peak[0:low, :] = jnp.maximum(peak[0:low, :], fold(past))
            past = jnp.max(past, axis=0, keepdims=True)
            past = jnp.transpose(jnp.broadcast_to(past, (LANES, high - low)))
            own = jnp.maximum(own, past)
        peak[low:high, :] = own

    steps_left = list(zip(SCORED[:-1], SCORED[1:]))
    for n in range(EARLY, CHUNKS):
        pass_rows(n)
        if n == TAGS_AFTER:
            tag_send[...] = merge_tile(0, tag_xs).reshape(SHARDS, 1, LANES)
            spread_rows(0, tag_send, tag_recv, ahead)
        if n in TURNS_AFTER:
            turn_rows(ORDER[TURNS_AFTER.index(n)])
        if n in SCORES_AFTER:
            if n == SCORES_AFTER[0]:
                tag_col, tag_row = member_tags()
            score(*steps_left.pop(0))
    for begin, end in steps_left:
        score(begin, end)
    best = jnp.max(peak[...], axis=1, keepdims=True)
    best = jnp.where(mine, best, -2.0)
    ret_send[...] = jnp.max(best.reshape(SHARDS, PAIR, LANES), axis=1, keepdims=True)

    spread_rows(1, ret_send, ret_recv, behind)
    rows_arrived(1, ret_recv)
    tiles[1] = jnp.transpose(ret_recv[...].reshape(SHARDS, LANES))[0:PAIR, :]
    spread_tile(1, ret_xs, -1)
    final = merge_tile(1, ret_xs)
    found = jnp.full((SHARDS, rows), -1.0, f32)
    for j in range(PAIR):
        found = jnp.maximum(found, jnp.where(hot[j] > 0.5, final[:, j : j + 1], -1.0))
    out_ref[...] = jnp.max(found, axis=0, keepdims=True)

    pltpu.make_async_copy(xsend, xsend, xs_sem).wait()
    pltpu.make_async_copy(ysend.at[others], ysend.at[others], ys_sem).wait()
    for n, held in enumerate((tag_xs, ret_xs)):
        pltpu.make_async_copy(held, held, tile_ss.at[n]).wait()
    for n, sent in enumerate((tag_send, ret_send)):
        pltpu.make_async_copy(sent.at[others], sent.at[others], row_ss.at[n]).wait()


def body(embeddings, cluster_id, row_targets):
    rows = embeddings.shape[0]
    features = embeddings.shape[1]
    copies = row_targets.shape[1]
    f32, bf16 = jnp.float32, jnp.bfloat16
    dma = pltpu.SemaphoreType.DMA

    def held(count):
        return pltpu.VMEM((count, PAIR, LANES), f32)

    small = pltpu.VMEM((SHARDS, 1, LANES), f32)

    out = pl.pallas_call(
        kernel,
        out_shape=jax.ShapeDtypeStruct((1, rows), f32),
        in_specs=[pl.BlockSpec(memory_space=pltpu.HBM)] * 3,
        out_specs=pl.BlockSpec(memory_space=pltpu.VMEM),
        scratch_shapes=[
            pltpu.VMEM((rows, features), bf16),
            pltpu.VMEM((1, rows), jnp.int32),
            pltpu.VMEM((copies, rows), jnp.int32),
            pltpu.VMEM((rows, features), bf16),
            pltpu.VMEM((PAIR, SHARDS, rows), bf16),
            pltpu.VMEM((CHUNKS, GROUPS - 1, CAP * CHUNK, features), bf16),
            pltpu.VMEM((CHUNKS, GROUPS, CAP * CHUNK, features), bf16),
            pltpu.VMEM((SHARDS, PAIR, features), bf16),
            pltpu.VMEM((SHARDS, PAIR, features), bf16),
            pltpu.VMEM((SHARDS, PAIR, features), bf16),
            held(2),
            held(GROUPS - 1),
            held(GROUPS - 1),
            small,
            small,
            small,
            small,
            pltpu.VMEM((SHARDS * PAIR, LANES), f32),
            dma((3,)),
            dma,
            dma((CHUNKS,)),
            dma,
            dma((CHUNKS,)),
            dma((2,)),
            dma((2,)),
            dma((2,)),
            dma((2,)),
        ],
        compiler_params=pltpu.CompilerParams(
            collective_id=0, has_side_effects=True, vmem_limit_bytes=63 * 2**20
        ),
        name="dedup",
    )(embeddings, cluster_id.reshape(1, rows), row_targets.T)
    return out.reshape(rows)


def solution(mesh):
    placed = (P(("shard", "grp"), None), P(("shard", "grp")), P(("shard", "grp"), None))
    return jax.shard_map(
        body, mesh=mesh, in_specs=placed, out_specs=P(("shard", "grp")), check_vma=False
    )
```

time: 225 us -> 71 us (0.32)
  Pallas kernels: 0 us -> 69.6 us
  local copies, waits for them, and re-layouts: 62.6 us -> 1.26 us
  blocking collectives: 49 us -> 0 us
  waiting for transfers between devices: 46.9 us -> 0 us
  starting transfers between devices: 35.9 us -> 0 us
  other arithmetic: 14.2 us -> 0 us
  between operations: 13.7 us -> 0.01 us
  matrix products: 2.27 us -> 0 us
    pallas_call x0 -> x1, Pallas kernels: none -> 69.6 us  [body(): pl.pallas_call(kernel, out_shape=jax.ShapeDtypeStruct((1, rows), f32), in...]
    all_to_all x3 -> x0, waiting for transfers between devices: 46.9 us -> none  [the longest x1 39.6 us: body(): lax.all_to_all(sent_rows.reshape(shards, groups * capacity, features), 's...]
    all_to_all x3 -> x0, starting transfers between devices: 35.9 us -> none  [the longest x1 21.9 us: body(): lax.all_to_all(sent_tags.reshape(shards, groups * capacity), 'shard', spl...]
    scatter x2 -> x0, local copies, waits for them, and re-layouts: 29.2 us -> none  [the longest x1 23 us: body(): source_row = jnp.full((bucket,), -1, jnp.int32).at[buffer_slot.reshape(-1...]
    all_gather x2 -> x0, blocking collectives: 29.1 us -> none  [the longest x1 21 us: body(): lax.all_gather(places, 'grp', axis=0, tiled=True)]
    gather x5 -> x0, local copies, waits for them, and re-layouts: 27.4 us -> none  [the longest x1 8.39 us: slot_places(): ordered = keyed[order]]
    all_to_all x1 -> x0, blocking collectives: 19.9 us -> none  [body(): lax.all_to_all(highest.reshape(shards, groups, capacity), 'shard', split_...]
    sort x1 -> x0, other arithmetic: 5.02 us -> none  [slot_places(): order = jnp.argsort(keyed, stable=True)]
  transfers between devices with their start and end apart: 4 -> 0, of which waited for: 3 -> 0; matrix products, arithmetic and copies ran while one was open for 28% -> 0% of each run, Pallas kernels for 0% -> 0%
where the time goes in v1:
time: 71 us; the launch traced here: 70.8 us
  Pallas kernels  69.6 us (98%)
  local copies, waits for them, and re-layouts  1.26 us (2%)
    pallas_call x1, Pallas kernels, body(): pl.pallas_call(kernel, out_shape=jax.ShapeDtypeStruct((1, rows), f32), in...  69.6 us

profile of v1, /device:TPU:1, one launch (start us, length us, event | category | flops | bytes accessed | tf_op | source)
XLA Modules:
  0.0 70.8 jit_solution(13375276945638111190)
XLA Ops:
  0.0 69.6 %dedup.1 = f32[1,512]{1,0:T(1,128)} custom-call(bf16[512,768]{1,0:T(8,128)(2,1)} %emb_hbm.1, s32[1,512]{1,0:T(1,128)} %bitcast.5, s32[3,512]{1,0:T(4,128)} %bitcast.3), custom_call_target="tpu_custom_call" | custom-call | tf_op jit(solution)/shard_map/dedup/pallas_call | solution.py:388
  69.6 1.3 %copy.5 = f32[512]{0:T(512)} copy(f32[512]{0:T(512)} %bitcast.4) | data formatting | bytes 4096

commit v2 on v1

--- a/solution.py
+++ b/solution.py
@@ -13,6 +13,8 @@
 CAP = 2
 PAIR = GROUPS * CAP
 LANES = 128
+PLANE = SHARDS // CORES
+LINES = GROUPS * CORES
 CHUNK = 16
 CHUNKS = SHARDS // CHUNK
 ORDER = (4, 5, 0, 1, 2, 3, 6, 7)
@@ -104,18 +106,13 @@
     def ahead(place):
         return at(*steps(place))
 
-    def behind(place):
-        dy, dz, dc = steps(place)
-        return at(-dy, -dz, dc)
-
-    def along(e):
-        return {"grp": (grp + e + GROUPS) % GROUPS}
+    def along(e, dc=0):
+        return {"shard": ys[0] + zs[0] + cs[dc], "grp": (grp + e + GROUPS) % GROUPS}
 
     barrier = pltpu.get_barrier_semaphore()
     for e in range(1, GROUPS):
-        pl.semaphore_signal(
-            barrier, inc=1, device_id=along(e), device_id_type=MESH
-        )
+        for dc in range(CORES):
+            pl.semaphore_signal(barrier, inc=1, device_id=along(e, dc), device_id_type=MESH)
     for place in range(1, SHARDS):
         pl.semaphore_signal(barrier, inc=1, device_id=ahead(place), device_id_type=MESH)
 
@@ -239,44 +236,55 @@
             copy.start()
 
     pack_rows(ORDER[: 2 * EARLY])
-    pl.semaphore_wait(barrier, SHARDS - 1 + GROUPS - 1)
+    pl.semaphore_wait(barrier, SHARDS - 1 + (GROUPS - 1) * CORES)
     for n in range(EARLY):
         send_rows(n)
     pack_rows(ORDER[2 * EARLY :])
 
-    row8 = lax.broadcasted_iota(jnp.int32, (PAIR, LANES), 0) // CAP
-
-    def spread_tile(n, held, sign):
-        for e in range(1, GROUPS):
+    def both_cores(block):
+        block = [
+            jnp.maximum(block[k * CHUNK : (k + 1) * CHUNK, :], block[(k + 1) * CHUNK : (k + 2) * CHUNK, :])
+            for k in range(0, CHUNKS, CORES)
+        ]
+        return jnp.concatenate(block, axis=0)
+
+    def spread_lines(n, plane, held, sign):
+        missing = jnp.zeros((LANES - PLANE, LANES), f32)
+        turned = jnp.transpose(jnp.concatenate([plane, missing], axis=0))
+        for m in range(LINES):
+            tiles[n, m] = turned[m * CAP : (m + 1) * CAP, :]
+        for m in range(1, LINES):
             pltpu.make_async_remote_copy(
-                src_ref=tiles.at[n],
-                dst_ref=held.at[e - 1],
+                src_ref=tiles.at[n, m],
+                dst_ref=held.at[m - 1],
                 send_sem=tile_ss.at[n],
                 recv_sem=tile_rs.at[n],
-                device_id=along(sign * e),
+                device_id=along(sign * (m % GROUPS), m // GROUPS),
                 device_id_type=MESH,
             ).start()
 
-    def merge_tile(n, held):
+    def merge_lines(n, held):
         pltpu.make_async_copy(held, held, tile_rs.at[n]).wait()
-        merged = tiles[n]
-        for e in range(1, GROUPS):
-            merged = jnp.where(row8 == e, held[e - 1], merged)
-        return jnp.transpose(
-            jnp.concatenate([merged, jnp.zeros((LANES - PAIR, LANES), f32)], axis=0)
-        )
-
-    others = pl.ds(1, SHARDS - 1)
-
-    def spread_rows(n, sent, held, device):
+        line = lax.broadcasted_iota(jnp.int32, (LANES, LANES), 0)
+        merged = jnp.zeros((LANES, LANES), f32)
+        for m in range(LINES):
+            lines = held[m - 1] if m else tiles[n, 0]
+            for r in range(CAP):
+                merged = jnp.where(line == m * CAP + r, lines[r : r + 1, :], merged)
+        return jnp.transpose(merged)[0:PLANE, :]
+
+    others = pl.ds(1, PLANE - 1)
+
+    def spread_rows(n, sent, held, sign):
         held[0] = sent[0]
-        for place in range(1, SHARDS):
+        for row in range(1, PLANE):
+            dy, dz, _ = steps(row // CHUNK * CORES * CHUNK + row % CHUNK)
             pltpu.make_async_remote_copy(
-                src_ref=sent.at[place],
-                dst_ref=held.at[place],
+                src_ref=sent.at[row],
+                dst_ref=held.at[row],
                 send_sem=row_ss.at[n],
                 recv_sem=row_rs.at[n],
-                device_id=device(place),
+                device_id=at(sign * dy, sign * dz, 0),
                 device_id_type=MESH,
             ).start()
 
@@ -286,23 +294,26 @@
     incoming[1].wait()
     cid = cid_ref[...].astype(f32) + 1.0
     lane = lax.broadcasted_iota(jnp.int32, (SHARDS, LANES), 1)
+    core_lane = lax.broadcasted_iota(jnp.int32, (SHARDS, LANES), 0) // CHUNK % CORES * PAIR
     tags = jnp.zeros((SHARDS, LANES), f32)
     for j in range(PAIR):
         tag = jnp.sum(hot[j].astype(f32) * cid, axis=1, keepdims=True)
-        tags = jnp.where(lane == j, tag, tags)
-    tiles[0] = jnp.transpose(tags)[0:PAIR, :] - 1.0
-    spread_tile(0, tag_xs, 1)
+        tags = jnp.where(lane == core_lane + j, tag, tags)
+    spread_lines(0, both_cores(tags) - 1.0, tag_xs, 1)
 
     total = SHARDS * PAIR
     lanes = lax.broadcasted_iota(jnp.int32, (total, LANES), 1)
     member = lax.broadcasted_iota(jnp.int32, (total, LANES), 0)
-    mine = lanes == member % PAIR
+    mine = lanes == member // (CHUNK * PAIR) % CORES * PAIR + member % PAIR
     number = lax.broadcasted_iota(jnp.int32, (total, 1), 0)
     column = lax.broadcasted_iota(jnp.int32, (1, total), 1)
 
     def member_tags():
         rows_arrived(0, tag_recv)
-        spread = jnp.broadcast_to(tag_recv[...], (SHARDS, PAIR, LANES)).reshape(total, LANES)
+        spread = jnp.broadcast_to(tag_recv[...], (PLANE, PAIR, LANES)).reshape(PLANE * PAIR, LANES)
+        block = CHUNK * PAIR
+        spread = [spread[k // CORES * block : (k // CORES + 1) * block, :] for k in range(CHUNKS)]
+        spread = jnp.concatenate(spread, axis=0)
         tag_col = jnp.sum(jnp.where(mine, spread, 0.0), axis=1, keepdims=True)
         tag_col = jnp.where(tag_col < 0.0, -2.0 - number.astype(f32), tag_col)
         return tag_col, jnp.transpose(jnp.broadcast_to(tag_col, (total, LANES)))[0:1, :]
@@ -341,8 +352,8 @@
     for n in range(EARLY, CHUNKS):
         pass_rows(n)
         if n == TAGS_AFTER:
-            tag_send[...] = merge_tile(0, tag_xs).reshape(SHARDS, 1, LANES)
-            spread_rows(0, tag_send, tag_recv, ahead)
+            tag_send[...] = merge_lines(0, tag_xs).reshape(PLANE, 1, LANES)
+            spread_rows(0, tag_send, tag_recv, 1)
         if n in TURNS_AFTER:
             turn_rows(ORDER[TURNS_AFTER.index(n)])
         if n in SCORES_AFTER:
@@ -353,20 +364,28 @@
         score(begin, end)
     best = jnp.max(peak[...], axis=1, keepdims=True)
     best = jnp.where(mine, best, -2.0)
-    ret_send[...] = jnp.max(best.reshape(SHARDS, PAIR, LANES), axis=1, keepdims=True)
-
-    spread_rows(1, ret_send, ret_recv, behind)
+    best = both_cores(jnp.max(best.reshape(SHARDS, PAIR, LANES), axis=1))
+    ret_send[...] = best.reshape(PLANE, 1, LANES)
+
+    spread_rows(1, ret_send, ret_recv, -1)
     rows_arrived(1, ret_recv)
-    tiles[1] = jnp.transpose(ret_recv[...].reshape(SHARDS, LANES))[0:PAIR, :]
-    spread_tile(1, ret_xs, -1)
-    final = merge_tile(1, ret_xs)
+    spread_lines(1, ret_recv[...].reshape(PLANE, LANES), ret_xs, -1)
+    final = merge_lines(1, ret_xs)
+    final = jnp.concatenate(
+        [
+            final[k // CORES * CHUNK : (k // CORES + 1) * CHUNK, k % CORES * PAIR : (k % CORES + 1) * PAIR]
+            for k in range(CHUNKS)
+        ],
+        axis=0,
+    )
     found = jnp.full((SHARDS, rows), -1.0, f32)
     for j in range(PAIR):
         found = jnp.maximum(found, jnp.where(hot[j] > 0.5, final[:, j : j + 1], -1.0))
     out_ref[...] = jnp.max(found, axis=0, keepdims=True)
 
     pltpu.make_async_copy(xsend, xsend, xs_sem).wait()
-    pltpu.make_async_copy(ysend.at[others], ysend.at[others], ys_sem).wait()
+    part = ysend.at[pl.ds(1, SHARDS - 1)]
+    pltpu.make_async_copy(part, part, ys_sem).wait()
     for n, held in enumerate((tag_xs, ret_xs)):
         pltpu.make_async_copy(held, held, tile_ss.at[n]).wait()
     for n, sent in enumerate((tag_send, ret_send)):
@@ -380,11 +399,8 @@
     f32, bf16 = jnp.float32, jnp.bfloat16
     dma = pltpu.SemaphoreType.DMA
 
-    def held(count):
-        return pltpu.VMEM((count, PAIR, LANES), f32)
-
-    small = pltpu.VMEM((SHARDS, 1, LANES), f32)
-
+    held = pltpu.VMEM((LINES - 1, CAP, LANES), f32)
+    small = pltpu.VMEM((PLANE, 1, LANES), f32)
     out = pl.pallas_call(
         kernel,
         out_shape=jax.ShapeDtypeStruct((1, rows), f32),
@@ -401,9 +417,9 @@
             pltpu.VMEM((SHARDS, PAIR, features), bf16),
             pltpu.VMEM((SHARDS, PAIR, features), bf16),
             pltpu.VMEM((SHARDS, PAIR, features), bf16),
-            held(2),
-            held(GROUPS - 1),
-            held(GROUPS - 1),
+            pltpu.VMEM((2, LINES, CAP, LANES), f32),
+            held,
+            held,
             small,
             small,
             small,

time: 71 us -> 71.2 us (level)
  no operation moved by 1% of the time
where the time goes in v2:
time: 71.2 us; the launch traced here: 71.1 us
  Pallas kernels  69.8 us (98%)
  local copies, waits for them, and re-layouts  1.26 us (2%)
    pallas_call x1, Pallas kernels, body(): pl.pallas_call(kernel, out_shape=jax.ShapeDtypeStruct((1, rows), f32), in...  69.8 us

profile of v2, /device:TPU:1, one launch (start us, length us, event | category | flops | bytes accessed | tf_op | source)
XLA Modules:
  0.0 71.1 jit_solution(12351092778100110434)
XLA Ops:
  0.0 69.8 %dedup.1 = f32[1,512]{1,0:T(1,128)} custom-call(bf16[512,768]{1,0:T(8,128)(2,1)} %emb_hbm.1, s32[1,512]{1,0:T(1,128)} %bitcast.5, s32[3,512]{1,0:T(4,128)} %bitcast.3), custom_call_target="tpu_custom_call" | custom-call | tf_op jit(solution)/shard_map/dedup/pallas_call | solution.py:404
  69.9 1.3 %copy.5 = f32[512]{0:T(512)} copy(f32[512]{0:T(512)} %bitcast.4) | data formatting | bytes 4096

commit v3 on v2

--- a/solution.py
+++ b/solution.py
@@ -177,14 +177,15 @@
     def x_copies(k):
         return [
             pltpu.make_async_remote_copy(
-                src_ref=xsend.at[k, e - 1, pl.ds(r * CHUNK, CHUNK)],
-                dst_ref=stage.at[k, e, pl.ds(r * CHUNK, CHUNK)],
+                src_ref=xsend.at[k, e - 1, pl.ds(r * CHUNK, CHUNK), columns],
+                dst_ref=stage.at[k, e, pl.ds(r * CHUNK, CHUNK), columns],
                 send_sem=xs_sem,
                 recv_sem=xr_sem.at[k],
                 device_id=along(e),
                 device_id_type=MESH,
             )
             for r in range(CAP)
+            for columns in (pl.ds(0, features // 2), pl.ds(features // 2, features // 2))
             for e in (1, 3, 2)
         ]
 
@@ -199,7 +200,7 @@
         part = (mid if k in ORDER[:EARLY] else recv).at[part]
         pltpu.make_async_copy(part, part, yr_sem.at[k]).wait()
 
-    def send_rows(n):
+    def send_rows(n, later):
         k = ORDER[n]
         copies = [
             pltpu.make_async_remote_copy(
@@ -212,10 +213,10 @@
             )
             for place in range(max(1, k * CHUNK), (k + 1) * CHUNK)
         ]
-        if n + EARLY < CHUNKS:
-            between = x_copies(ORDER[n + EARLY])
-            for m, copy in enumerate(between):
-                copies.insert(m + (m + 1) * CHUNK // (len(between) + 1), copy)
+        between = [copy for m in later if m < CHUNKS for copy in x_copies(ORDER[m])]
+        alone = len(copies)
+        for m, copy in enumerate(between):
+            copies.insert(m + (m + 1) * alone // (len(between) + 1), copy)
         for copy in copies:
             copy.start()
 
@@ -224,7 +225,7 @@
         ysend[k * CHUNK : (k + 1) * CHUNK] = x_arrived(k)
         if k == 0:
             recv[0] = ysend[0]
-        send_rows(n)
+        send_rows(n, [n + EARLY])
 
     def turn_rows(k):
         yz_arrived(k)
@@ -235,11 +236,12 @@
         for copy in x_copies(k):
             copy.start()
 
-    pack_rows(ORDER[: 2 * EARLY])
+    pack_rows(ORDER[:1])
     pl.semaphore_wait(barrier, SHARDS - 1 + (GROUPS - 1) * CORES)
-    for n in range(EARLY):
-        send_rows(n)
-    pack_rows(ORDER[2 * EARLY :])
+    send_rows(0, [])
+    pack_rows(ORDER[1:4])
+    send_rows(1, [2, 3])
+    pack_rows(ORDER[4:])
 
     def both_cores(block):
         block = [

time: 71.2 us -> 71.4 us (level)
  no operation moved by 1% of the time
where the time goes in v3:
time: 71.4 us; the launch traced here: 71.3 us
  Pallas kernels  70 us (98%)
  local copies, waits for them, and re-layouts  1.26 us (2%)
    pallas_call x1, Pallas kernels, body(): pl.pallas_call(kernel, out_shape=jax.ShapeDtypeStruct((1, rows), f32), in...  70 us

profile of v3, /device:TPU:1, one launch (start us, length us, event | category | flops | bytes accessed | tf_op | source)
XLA Modules:
  0.0 71.3 jit_solution(2443681980217822565)
XLA Ops:
  0.0 70.0 %dedup.1 = f32[1,512]{1,0:T(1,128)} custom-call(bf16[512,768]{1,0:T(8,128)(2,1)} %emb_hbm.1, s32[1,512]{1,0:T(1,128)} %bitcast.5, s32[3,512]{1,0:T(4,128)} %bitcast.3), custom_call_target="tpu_custom_call" | custom-call | tf_op jit(solution)/shard_map/dedup/pallas_call | solution.py:406
  70.0 1.3 %copy.5 = f32[512]{0:T(512)} copy(f32[512]{0:T(512)} %bitcast.4) | data formatting | bytes 4096

commit v4 on v3

--- a/solution.py
+++ b/solution.py
@@ -17,11 +17,10 @@
 LINES = GROUPS * CORES
 CHUNK = 16
 CHUNKS = SHARDS // CHUNK
-ORDER = (4, 5, 0, 1, 2, 3, 6, 7)
-EARLY = 2
-TAGS_AFTER = 3
-TURNS_AFTER = (4, 5)
-SCORES_AFTER = (6, 7)
+ORDER = (2, 3, 4, 5, 0, 1, 6, 7)
+EARLY = 4
+TURNS = {4: [], 5: [0], 6: [1], 7: [2, 3]}
+TAGS_AFTER = 5
 SCORED = (0, 32, 64, 96, 112, 128)
 
 
@@ -177,15 +176,14 @@
     def x_copies(k):
         return [
             pltpu.make_async_remote_copy(
-                src_ref=xsend.at[k, e - 1, pl.ds(r * CHUNK, CHUNK), columns],
-                dst_ref=stage.at[k, e, pl.ds(r * CHUNK, CHUNK), columns],
+                src_ref=xsend.at[k, e - 1, pl.ds(r * CHUNK, CHUNK)],
+                dst_ref=stage.at[k, e, pl.ds(r * CHUNK, CHUNK)],
                 send_sem=xs_sem,
                 recv_sem=xr_sem.at[k],
                 device_id=along(e),
                 device_id_type=MESH,
             )
             for r in range(CAP)
-            for columns in (pl.ds(0, features // 2), pl.ds(features // 2, features // 2))
             for e in (1, 3, 2)
         ]
 
@@ -213,19 +211,19 @@
             )
             for place in range(max(1, k * CHUNK), (k + 1) * CHUNK)
         ]
-        between = [copy for m in later if m < CHUNKS for copy in x_copies(ORDER[m])]
+        between = [copy for m in later for copy in x_copies(ORDER[m])]
         alone = len(copies)
         for m, copy in enumerate(between):
             copies.insert(m + (m + 1) * alone // (len(between) + 1), copy)
         for copy in copies:
             copy.start()
 
-    def pass_rows(n):
+    def pass_rows(n, later):
         k = ORDER[n]
         ysend[k * CHUNK : (k + 1) * CHUNK] = x_arrived(k)
         if k == 0:
             recv[0] = ysend[0]
-        send_rows(n, [n + EARLY])
+        send_rows(n, later)
 
     def turn_rows(k):
         yz_arrived(k)
@@ -233,15 +231,12 @@
         block = jnp.dot(back, block, preferred_element_type=f32).astype(bf16)
         for j in range(PAIR):
             keep_for_x(k, j, block[j * CHUNK : (j + 1) * CHUNK, :])
-        for copy in x_copies(k):
-            copy.start()
-
-    pack_rows(ORDER[:1])
-    pl.semaphore_wait(barrier, SHARDS - 1 + (GROUPS - 1) * CORES)
-    send_rows(0, [])
-    pack_rows(ORDER[1:4])
-    send_rows(1, [2, 3])
-    pack_rows(ORDER[4:])
+
+    for n in range(EARLY):
+        pack_rows([ORDER[n], ORDER[n + EARLY]])
+        if n == 0:
+            pl.semaphore_wait(barrier, SHARDS - 1 + (GROUPS - 1) * CORES)
+        send_rows(n, [n + EARLY])
 
     def both_cores(block):
         block = [
@@ -350,19 +345,15 @@
             own = jnp.maximum(own, past)
         peak[low:high, :] = own
 
-    steps_left = list(zip(SCORED[:-1], SCORED[1:]))
     for n in range(EARLY, CHUNKS):
-        pass_rows(n)
+        for m in TURNS[n]:
+            turn_rows(ORDER[m])
+        pass_rows(n, TURNS[n])
         if n == TAGS_AFTER:
             tag_send[...] = merge_lines(0, tag_xs).reshape(PLANE, 1, LANES)
             spread_rows(0, tag_send, tag_recv, 1)
-        if n in TURNS_AFTER:
-            turn_rows(ORDER[TURNS_AFTER.index(n)])
-        if n in SCORES_AFTER:
-            if n == SCORES_AFTER[0]:
-                tag_col, tag_row = member_tags()
-            score(*steps_left.pop(0))
-    for begin, end in steps_left:
+    tag_col, tag_row = member_tags()
+    for begin, end in zip(SCORED[:-1], SCORED[1:]):
         score(begin, end)
     best = jnp.max(peak[...], axis=1, keepdims=True)
     best = jnp.where(mine, best, -2.0)

time: 71.4 us -> 72.5 us (1.015)
  Pallas kernels: 70 us -> 71.1 us
    pallas_call x1, Pallas kernels: 70 us -> 71.1 us  [body(): pl.pallas_call(kernel, out_shape=jax.ShapeDtypeStruct((1, rows), f32), in...]
where the time goes in v4:
time: 72.5 us; the launch traced here: 72.4 us
  Pallas kernels  71.1 us (98%)
  local copies, waits for them, and re-layouts  1.26 us (2%)
    pallas_call x1, Pallas kernels, body(): pl.pallas_call(kernel, out_shape=jax.ShapeDtypeStruct((1, rows), f32), in...  71.1 us

profile of v4, /device:TPU:1, one launch (start us, length us, event | category | flops | bytes accessed | tf_op | source)
XLA Modules:
  0.0 72.4 jit_solution(11167088602210105766)
XLA Ops:
  0.0 71.1 %dedup.1 = f32[1,512]{1,0:T(1,128)} custom-call(bf16[512,768]{1,0:T(8,128)(2,1)} %emb_hbm.1, s32[1,512]{1,0:T(1,128)} %bitcast.5, s32[3,512]{1,0:T(4,128)} %bitcast.3), custom_call_target="tpu_custom_call" | custom-call | tf_op jit(solution)/shard_map/dedup/pallas_call | solution.py:397
  71.1 1.3 %copy.5 = f32[512]{0:T(512)} copy(f32[512]{0:T(512)} %bitcast.4) | data formatting | bytes 4096

commit v5 on v1

--- a/solution.py
+++ b/solution.py
@@ -38,10 +38,10 @@
     return (dy + SIDE) % SIDE, (dz + 2 * SIDE) % SIDE, chunk % CORES
 
 
-def shard_at(me, place, sign):
+def shard_at(me, place, way):
     dy, dz, dc = steps(place)
-    y = (me // (SIDE * CORES) + sign * dy + SIDE) % SIDE
-    z = ((me // CORES) % SIDE + sign * dz + SIDE) % SIDE
+    y = (me // (SIDE * CORES) + way * dy + SIDE) % SIDE
+    z = ((me // CORES) % SIDE + way * dz + SIDE) % SIDE
     c = (me + dc) % CORES
     return (y * SIDE + z) * CORES + c
 
@@ -94,8 +94,9 @@
     for copy in incoming:
         copy.start()
 
-    ys = [(me // (SIDE * CORES) + d) % SIDE * (SIDE * CORES) for d in range(SIDE)]
-    zs = [(me // CORES + d) % SIDE * CORES for d in range(SIDE)]
+    way = 1 - me % CORES * 2
+    ys = [(me // (SIDE * CORES) + way * d + SIDE) % SIDE * (SIDE * CORES) for d in range(SIDE)]
+    zs = [(me // CORES + way * d + SIDE) % SIDE * CORES for d in range(SIDE)]
     cs = [(me + d) % CORES for d in range(CORES)]
 
     def at(dy, dz, dc):
@@ -106,7 +107,7 @@
 
     def behind(place):
         dy, dz, dc = steps(place)
-        return at(-dy, -dz, dc)
+        return at(dy, dz, dc) if dc else at(-dy, -dz, dc)
 
     def along(e):
         return {"grp": (grp + e + GROUPS) % GROUPS}
@@ -120,7 +121,7 @@
         pl.semaphore_signal(barrier, inc=1, device_id=ahead(place), device_id_type=MESH)
 
     place = lax.broadcasted_iota(jnp.int32, (SHARDS, 1), 0)
-    peers = shard_at(me, place, 1) * GROUPS
+    peers = shard_at(me, place, way) * GROUPS
     before = lax.broadcasted_iota(jnp.int32, (rows, rows), 0) < lax.broadcasted_iota(
         jnp.int32, (rows, rows), 1
     )

time: 71 us -> 70.8 us (level)
  no operation moved by 1% of the time
where the time goes in v5:
time: 70.8 us; the launch traced here: 70.7 us
  Pallas kernels  69.4 us (98%)
  local copies, waits for them, and re-layouts  1.26 us (2%)
    pallas_call x1, Pallas kernels, body(): pl.pallas_call(kernel, out_shape=jax.ShapeDtypeStruct((1, rows), f32), in...  69.4 us

profile of v5, /device:TPU:1, one launch (start us, length us, event | category | flops | bytes accessed | tf_op | source)
XLA Modules:
  0.0 70.7 jit_solution(3227640015296439706)
XLA Ops:
  0.0 69.4 %dedup.1 = f32[1,512]{1,0:T(1,128)} custom-call(bf16[512,768]{1,0:T(8,128)(2,1)} %emb_hbm.1, s32[1,512]{1,0:T(1,128)} %bitcast.5, s32[3,512]{1,0:T(4,128)} %bitcast.3), custom_call_target="tpu_custom_call" | custom-call | tf_op jit(solution)/shard_map/dedup/pallas_call | solution.py:389
  69.5 1.3 %copy.5 = f32[512]{0:T(512)} copy(f32[512]{0:T(512)} %bitcast.4) | data formatting | bytes 4096

commit v6 on v2

--- a/solution.py
+++ b/solution.py
@@ -19,9 +19,7 @@
 CHUNKS = SHARDS // CHUNK
 ORDER = (4, 5, 0, 1, 2, 3, 6, 7)
 EARLY = 2
-TAGS_AFTER = 3
-TURNS_AFTER = (4, 5)
-SCORES_AFTER = (6, 7)
+TAGS_AFTER = 5
 SCORED = (0, 32, 64, 96, 112, 128)
 
 
@@ -348,19 +346,15 @@
             own = jnp.maximum(own, past)
         peak[low:high, :] = own
 
-    steps_left = list(zip(SCORED[:-1], SCORED[1:]))
     for n in range(EARLY, CHUNKS):
         pass_rows(n)
         if n == TAGS_AFTER:
             tag_send[...] = merge_lines(0, tag_xs).reshape(PLANE, 1, LANES)
             spread_rows(0, tag_send, tag_recv, 1)
-        if n in TURNS_AFTER:
-            turn_rows(ORDER[TURNS_AFTER.index(n)])
-        if n in SCORES_AFTER:
-            if n == SCORES_AFTER[0]:
-                tag_col, tag_row = member_tags()
-            score(*steps_left.pop(0))
-    for begin, end in steps_left:
+    for n in range(EARLY):
+        turn_rows(ORDER[n])
+    tag_col, tag_row = member_tags()
+    for begin, end in zip(SCORED[:-1], SCORED[1:]):
         score(begin, end)
     best = jnp.max(peak[...], axis=1, keepdims=True)
     best = jnp.where(mine, best, -2.0)

time: 71.2 us -> 71.2 us (level)
  no operation moved by 1% of the time
where the time goes in v6:
time: 71.2 us; the launch traced here: 71.1 us
  Pallas kernels  69.8 us (98%)
  local copies, waits for them, and re-layouts  1.26 us (2%)
    pallas_call x1, Pallas kernels, body(): pl.pallas_call(kernel, out_shape=jax.ShapeDtypeStruct((1, rows), f32), in...  69.8 us

profile of v6, /device:TPU:1, one launch (start us, length us, event | category | flops | bytes accessed | tf_op | source)
XLA Modules:
  0.0 71.1 jit_solution(5761135580754971448)
XLA Ops:
  0.0 69.8 %dedup.1 = f32[1,512]{1,0:T(1,128)} custom-call(bf16[512,768]{1,0:T(8,128)(2,1)} %emb_hbm.1, s32[1,512]{1,0:T(1,128)} %bitcast.5, s32[3,512]{1,0:T(4,128)} %bitcast.3), custom_call_target="tpu_custom_call" | custom-call | tf_op jit(solution)/shard_map/dedup/pallas_call | solution.py:398
  69.8 1.3 %copy.5 = f32[512]{0:T(512)} copy(f32[512]{0:T(512)} %bitcast.4) | data formatting | bytes 4096
